TPU v7x, 512 devices: a whole 4x8x8 slice. The times are simulated.
512 devices in a mesh: out: 16 (over y, core), in: 32 (over z, x).
Axes of the slice: x: 4, y: 8, z: 8, core: 2. Of those that a mesh axis runs over, the one named last changes fastest.
Arguments:
- weight: float32 [16384, 16384], P('out', 'in'), may hold values from -6 to 6
- keep_tiles: int32 [128, 128], P('out', 'in'), may hold values from 0 to 1, as said below
- factor_rows: float32 [4, 256, 16384], P(None, 'out', 'in'), may hold values from -0.375 to 0.375
- diag_inverse: float32 [16384], P('in'), may hold values from 0.5 to 2
- block_order: int32 [4], replicated, may hold values from 0 to 63, as said below
Outputs:
- pruned_weight: float32 [16384, 16384], P('out', 'in')
Inputs may be any that keep to these rules, and one draw needn't show every extreme that they name: `block_order`: distinct block numbers; the first and the last block are always among them. `keep_tiles`: for each index of out and each block of 256 inputs, the group of 16 tiles holds at most 10 zeros; in every block some group holds exactly 10.
All inputs are finite; a program needn't handle non-finite values.
Results may differ from a plain program's by a relative error of at most 0.0001.
Values sent between devices are 32-bit elements; how exact they have to be, the bound alone decides.
A program may use at most 64 MiB of HBM per device.

v0:
```python
import jax
import jax.numpy as jnp
from jax import lax
from jax.sharding import PartitionSpec as P

TILE = 128
NBLK = 4


def from_root(array, axis, root):
    mine = lax.axis_index(axis) == root
    return lax.psum(jnp.where(mine, array, jnp.zeros_like(array)), axis)


def expand_keep(flags):
    return jnp.repeat(jnp.repeat(flags, TILE, 0), TILE, 1)


def body(weight, keep_tiles, factor_rows, diag_inverse, block_order):
    rows, cols = weight.shape
    block = 2 * TILE
    per_device = cols // block
    col_ids = lax.axis_index("in") * cols + jnp.arange(cols, dtype=jnp.int32)
    col_block = col_ids // block
    keep_full = expand_keep(keep_tiles).astype(jnp.float32)
    panel_all = lax.all_gather(factor_rows, "out", axis=1, tiled=True)
    for step in range(NBLK):
        panel = panel_all[step]
        chosen_block = block_order[step]
        owner = chosen_block // per_device
        offset = chosen_block % per_device * block
        block_w = lax.dynamic_slice_in_dim(weight, offset, block, 1)
        block_keep = lax.dynamic_slice_in_dim(keep_full, offset, block, 1)
        scales = lax.dynamic_slice_in_dim(diag_inverse, offset, block, 0)
        errors = block_w * (1.0 - block_keep) * scales[None, :]
        errors = from_root(errors, "in", owner)
        update = jnp.dot(
            errors, panel, preferred_element_type=jnp.float32, precision=lax.Precision.HIGHEST
        )
        finished = jnp.any(col_block[:, None] == block_order[None, : step + 1], axis=1)
        weight = weight - jnp.where(finished[None, :], jnp.float32(0.0), update)
    processed = jnp.any(col_block[:, None] == block_order[None, :], axis=1)
    return jnp.where(processed[None, :], weight * keep_full, weight)


def solution(mesh):
    return jax.shard_map(
        body,
        mesh=mesh,
        in_specs=(P("out", "in"), P("out", "in"), P(None, "out", "in"), P("in"), P()),
        out_specs=P("out", "in"),
        check_vma=False,
    )
```

profile of v0, /device:TPU:1, one launch (start us, length us, event | category | flops | bytes accessed | tf_op | source)
XLA Modules:
  0.0 693.0 jit_solution(3402120489849063699)
XLA Ops:
  7.4 1.5 fusion.4
  17.3 0.7 convert_element_type.11
  18.0 0.1 copy.7
  18.1 1.2 broadcast_in_dim.65
  19.4 1.5 copy.12
  20.9 0.1 fusion.3
  21.0 2.7 multiply_select_fusion.4
  23.6 0.0 all-reduce.5.cloned.1.call-update
  23.6 0.0 all-gather.2.cloned.1.call-start
  23.7 0.5 all-gather.2.cloned.1.call-update
  24.2 0.0 all-reduce.7.cloned.1.call-start
  25.0 0.6 broadcast_compare_fusion
  25.6 160.0 %all-reduce.5.cloned.1.call-done = f32[1024,256]{1,0:T(8,128)} async-done(((f32[1024,256]{1,0:T(8,128)}), f32[1024,256]{1,0:T(8,128)}) %all-reduce.5.cloned.1.call-update) | async-done | bytes 1048592 | tf_op jit(solution)/shard_map/psum | solution.py:12
  185.6 4.1 select_subtract_fusion.2
  189.8 1.3 copy-done.4
  191.1 1.3 multiply_select_fusion.3
  192.4 0.0 all-reduce.9.cloned.1.call-start
  193.1 0.1 compare_reduce_fusion.1
  193.2 157.3 %all-reduce.7.cloned.1.call-done = f32[1024,256]{1,0:T(8,128)} async-done(((f32[1024,256]{1,0:T(8,128)}), f32[1024,256]{1,0:T(8,128)}) %all-reduce.7.cloned.1.call-update) | async-done | bytes 1048592 | tf_op jit(solution)/shard_map/psum | solution.py:12
  350.5 4.1 select_subtract_fusion.1
  354.6 1.3 copy-done.3
  356.0 1.3 multiply_select_fusion.2
  357.3 0.0 all-reduce.11.cloned.1.call-start
  358.0 0.1 compare_reduce_fusion
  358.1 157.4 %all-reduce.9.cloned.1.call-done = f32[1024,256]{1,0:T(8,128)} async-done(((f32[1024,256]{1,0:T(8,128)}), f32[1024,256]{1,0:T(8,128)}) %all-reduce.9.cloned.1.call-update) | async-done | bytes 1048592 | tf_op jit(solution)/shard_map/psum | solution.py:12
  515.5 4.1 select_subtract_fusion
  519.6 1.3 copy-done.5
  520.9 1.2 multiply_select_fusion.1
  522.2 0.0 all-reduce.11.cloned.1.call-update
  522.2 0.1 compare_reduce_fusion.2
  522.3 158.2 %all-reduce.11.cloned.1.call-done = f32[1024,256]{1,0:T(8,128)} async-done(((f32[1024,256]{1,0:T(8,128)}), f32[1024,256]{1,0:T(8,128)}) %all-reduce.11.cloned.1.call-update) | async-done | bytes 1048592 | tf_op jit(solution)/shard_map/psum | solution.py:12
  680.4 5.4 multiply_select_fusion
  (19 shorter events, 0.1 us)
Async XLA Ops:
  7.4 178.3 %all-reduce.5.cloned.1.call-start = ((), (), s32[]{:S(2)}) async-start(), calls=%async_computation | async-start | bytes 2097152 | tf_op jit(solution)/shard_map/psum | solution.py:12
  19.4 1.5 copy-start.7
  23.6 162.0 %all-gather.2.cloned.1.call-start = ((), (), s32[]{:S(2)}) async-start(), calls=%async_computation.1 | async-start | bytes 2228224 | tf_op jit(solution)/shard_map/all_gather | solution.py:26
  24.2 326.3 %all-reduce.7.cloned.1.call-start = ((), (), s32[]{:S(2)}) async-start(), calls=%async_computation.2 | async-start | bytes 2097152 | tf_op jit(solution)/shard_map/psum | solution.py:12
  185.6 5.5 copy-start
  189.8 1.3 copy-start.4
  191.1 2.0 copy-start.6
  192.4 323.1 %all-reduce.9.cloned.1.call-start = ((), (), s32[]{:S(2)}) async-start(), calls=%async_computation.3 | async-start | bytes 2097152 | tf_op jit(solution)/shard_map/psum | solution.py:12
  350.5 5.5 copy-start.1
  354.6 1.3 copy-start.3
  357.3 323.2 %all-reduce.11.cloned.1.call-start = ((), (), s32[]{:S(2)}) async-start(), calls=%async_computation.4 | async-start | bytes 2097152 | tf_op jit(solution)/shard_map/psum | solution.py:12
  515.5 5.5 copy-start.2
  519.6 1.3 copy-start.5
Sparse Core Ops, SparseCore 0:
  23.8 161.8 all-reduce.4
  192.5 157.9 all-reduce.6
  357.4 158.0 all-reduce.8
  522.3 158.0 all-reduce.10
Sparse Core Ops, SparseCore 1:
  26.3 48.0 all-gather.1
where the time goes:
time: 697 us; the launch traced here: 693 us
  waiting for transfers between devices  633 us (91%)
  between operations  25.2 us (4%)
  matrix products  17.8 us (3%)
  local copies, waits for them, and re-layouts  8.32 us (1%)
  other arithmetic  8.03 us (1%)
    psum x4, waiting for transfers between devices, from_root(): return lax.psum(jnp.where(mine, array, jnp.zeros_like(array)), axis)  633 us
    dot_general x4, matrix products, body(): jnp.dot(errors, panel, preferred_element_type=jnp.float32, precision=lax....  17.8 us
  transfers between devices with their start and end apart: 5, of which 4 were waited for; matrix products, arithmetic and copies ran while one was open for 0% of the time, Pallas kernels for 0%

commit v1 on v0

v1 whole, which is shorter than its diff:
```python
import jax
import jax.numpy as jnp
from jax import lax
from jax.experimental import pallas as pl
from jax.experimental.pallas import tpu as pltpu
from jax.sharding import PartitionSpec as P

MESH = pl.DeviceIdType.MESH
TILE = 128
NBLK = 4
MAXP = 10
NZ, NX, NY = 8, 4, 8
NIN, NOUT = NZ * NX, NY * 2
ROWS = MAXP * TILE
CH = ROWS // NIN
PAIRS = [(j, k) for k in range(NBLK) for j in range(k)]
GROWS = len(PAIRS) * 4
F32 = jnp.float32
NEAR = (1, 7, 2, 6, 3, 5, 4)


def wait_for(ref, sem):
    pltpu.make_async_copy(ref, ref, sem).wait()


def stage(bo_ref, keep_ref, w_hbm, f_ref, d_ref, m_out, ce_out, gc_ref, wb, sem):
    me = lax.axis_index("in")
    last = NIN - 1
    blk = 2 * TILE
    first_b, last_b = 0, 2 * NIN - 1
    bo = [bo_ref[k] for k in range(NBLK)]
    mid = [jnp.int32(0), jnp.int32(0)]
    seen = jnp.int32(0)
    for k in range(NBLK):
        is_mid = jnp.logical_and(bo[k] != first_b, bo[k] != last_b)
        for q in range(2):
            mid[q] = jnp.where(jnp.logical_and(is_mid, seen == q), bo[k], mid[q])
        seen = seen + is_mid.astype(jnp.int32)
    is_root = jnp.logical_or(me == 0, me == last)
    jobs = [
        (mid[0] // 2 == me, mid[0] % 2, m_out.at[0]),
        (mid[1] // 2 == me, mid[1] % 2, m_out.at[1]),
        (is_root, jnp.where(me == last, 1, 0), ce_out),
    ]

    def fetch(i):
        half = pl.ds(pl.multiple_of(jobs[i][1] * blk, blk), blk)
        return pltpu.make_async_copy(w_hbm.at[:, half], wb.at[i], sem.at[i])

    for i, (own, lb, out) in enumerate(jobs):
        @pl.when(own)
        def _():
            fetch(i).start()

    gc_ref[pl.ds(GROWS, NIN - GROWS)] = jnp.zeros((NIN - GROWS, 8, TILE), F32)
    row = lax.broadcasted_iota(jnp.int32, (8, TILE), 0)
    lane = lax.broadcasted_iota(jnp.int32, (8, TILE), 1)
    for k in range(NBLK):
        own = bo[k] // 2 == me

        @pl.when(own)
        def _():
            off = pl.multiple_of((bo[k] % 2) * blk, blk)
            cb = (bo[k] % 2) * 2
            flags = jnp.zeros((8, TILE), F32)
            for tt in range(16):
                pr = (1 - keep_ref[cb + tt % 2, tt // 2]).astype(F32)
                flags = jnp.where(jnp.logical_and(row == k, lane == tt), pr, flags)
            gc_ref[GROWS] = gc_ref[GROWS] + flags
            for half in range(2):
                d = d_ref[0:1, pl.ds(pl.multiple_of(off + half * TILE, TILE), TILE)]
                gc_ref[GROWS + 1, pl.ds(2 * k + half, 1), :] = d

        for p, (j, kk) in enumerate(PAIRS):
            if kk != k:
                continue

            @pl.when(own)
            def _():
                for half in range(2):
                    cols = pl.ds(pl.multiple_of((bo[k] % 2) * blk + half * TILE, TILE), TILE)
                    d = d_ref[0:1, cols]
                    for rh in range(2):
                        gc_ref[p * 4 + half * 2 + rh] = f_ref[j, pl.ds(rh * 8, 8), cols] * d

            @pl.when(jnp.logical_not(own))
            def _():
                gc_ref[pl.ds(p * 4, 4)] = jnp.zeros((4, 8, TILE), F32)

    for i, (own, lb, out) in enumerate(jobs):
        if i < 2:
            out[...] = jnp.zeros((ROWS, TILE), F32)

        @pl.when(own)
        def _():
            if i == 2:
                out[...] = jnp.zeros((ROWS, TILE), F32)
            fetch(i).wait()
            cnt = jnp.int32(0)
            for tt in range(16):
                r, cc = tt // 2, tt % 2
                pr = 1 - keep_ref[lb * 2 + cc, r]

                @pl.when(pr == 1)
                def _():
                    rows = pl.ds(pl.multiple_of(cnt * TILE, TILE), TILE)
                    out[rows, :] = wb[i, r * TILE : (r + 1) * TILE, cc * TILE : (cc + 1) * TILE]

                cnt = jnp.minimum(cnt + pr, MAXP - 1 if tt == 15 else MAXP)


def exchange(m, ce, gc_hbm, f_hbm, t_out, f_out, g_out, fl_out,
             t, mq, gc, rb1, sb2, rb2, grb, gf,
             loc, fl_sem, out_sem, f_s, f_r, fc_s, fc_r, g_s, g_r, gc_s, gc_r, grs_s, grs_r, gag_s, gag_r,
             sc_s, sc_r, r1_s, r1_r, r2_s, r2_r, a1e_s, a1e_r, a2e_s, a2e_r, a1m_s, a1m_r, a2m_s, a2m_r):
    o = lax.axis_index("out")
    me = lax.axis_index("in")
    y, c = o // 2, o % 2
    z, x = me // NX, me % NX
    last = NIN - 1
    is_root = jnp.logical_or(me == 0, me == last)

    gcopy = pltpu.make_async_copy(gc_hbm, gc, loc.at[0])
    gcopy.start()
    mcopy = pltpu.make_async_copy(m.at[:, :, pl.ds(pl.multiple_of(x * CH, 8), CH)], mq, loc.at[1])
    mcopy.start()
    fown = pltpu.make_async_copy(f_hbm, f_out.at[o], loc.at[2])
    fown.start()

    def ydev(dy):
        return (lax.rem(y + dy, NY) * 2 + c, me)

    def zdev(dz):
        return (o, lax.rem(z + dz, NZ) * NX + x)

    def xdev(dx):
        return (o, z * NX + lax.rem(x + dx, NX))

    other = (y * 2 + 1 - c, me)

    def send(src, dst, ssem, rsem, dev):
        pltpu.make_async_remote_copy(
            src_ref=src, dst_ref=dst, send_sem=ssem, recv_sem=rsem, device_id=dev, device_id_type=MESH
        ).start()

    barrier = pltpu.get_barrier_semaphore()

    def greet(r, _):
        pl.semaphore_signal(barrier, inc=1, device_id=(o, lax.rem(me + r, NIN)), device_id_type=MESH)
        return 0

    lax.fori_loop(1, NIN, greet, 0)
    for dy in range(1, NY):
        pl.semaphore_signal(barrier, inc=1, device_id=ydev(dy), device_id_type=MESH)
    pl.semaphore_signal(barrier, inc=1, device_id=other, device_id_type=MESH)
    pl.semaphore_wait(barrier, NIN - 1 + NY - 1 + 1)

    gcopy.wait()

    def spread_g(r, _):
        peer = lax.rem(me + r, NIN)
        send(gc.at[peer], grb.at[r], grs_s, grs_r, (o, peer))
        return 0

    lax.fori_loop(1, NIN, spread_g, 0)

    for dz in NEAR + (0,):
        for dx in range(1, NX):
            part = pl.ds(pl.multiple_of(lax.rem(x + dx, NX) * CH, 8), CH)
            send(m.at[:, lax.rem(z + dz, NZ), part], rb1.at[dz, dx - 1], r1_s, r1_r.at[dz], xdev(dx))

    for e in range(2):
        root = e * last

        @pl.when(me == root)
        def _():
            def scatter(r, _):
                peer = lax.rem(me + r, NIN)
                rows = pl.ds(pl.multiple_of(peer * CH, 8), CH)
                send(ce.at[rows], t.at[e, rows], sc_s, sc_r.at[e], (o, peer))
                return 0

            lax.fori_loop(1, NIN, scatter, 0)

    for dy in NEAR:
        send(f_hbm, f_out.at[o], f_s, f_r.at[dy - 1], ydev(dy))
    send(f_hbm, f_out.at[o], fc_s, fc_r, other)

    mine = pl.ds(pl.multiple_of(me * CH, 8), CH)

    wait_for(grb.at[pl.ds(1, NIN - 1)], grs_r)
    grb[0] = gc[me]
    gf[me] = jnp.sum(grb[...], axis=0)

    def back_g(r, _):
        send(gf.at[me], gf.at[me], gag_s, gag_r, (o, lax.rem(me + r, NIN)))
        return 0

    lax.fori_loop(1, NIN, back_g, 0)

    for e in range(2):
        root = e * last

        @pl.when(me == root)
        def _():
            own = pltpu.make_async_copy(ce.at[mine], t.at[e, mine], loc.at[4])
            own.start()
            own.wait()

        @pl.when(me != root)
        def _():
            wait_for(t.at[e, mine], sc_r.at[e])

    for dz in NEAR:
        send(t.at[pl.ds(0, 2), mine], t.at[pl.ds(0, 2), mine], a1e_s, a1e_r.at[dz - 1], zdev(dz))
    for dx in range(1, NX):
        send(t.at[pl.ds(0, 2), mine], t.at[pl.ds(0, 2), mine], a2e_s, a2e_r, xdev(dx))

    mcopy.wait()
    for dz in NEAR + (0,):
        wait_for(rb1.at[dz], r1_r.at[dz])
        acc = mq[:, lax.rem(z + dz, NZ)]
        for q in range(NX - 1):
            acc = acc + rb1[dz, q]
        sb2[dz] = acc
        if dz:
            send(sb2.at[dz], rb2.at[dz - 1], r2_s, r2_r, zdev(dz))

    for dz in NEAR:
        h = lax.rem(z + NZ - dz, NZ) * NX + x
        rows = pl.ds(pl.multiple_of(h * CH, 8), CH)
        wait_for(t.at[pl.ds(0, 2), rows], a1e_r.at[dz - 1])
        for dx in range(1, NX):
            send(t.at[pl.ds(0, 2), rows], t.at[pl.ds(0, 2), rows], a2e_s, a2e_r, xdev(dx))

    wait_for(gf.at[pl.ds(1, NIN - 1)], gag_r)
    gown = pltpu.make_async_copy(gf.at[pl.ds(0, GROWS)], g_out.at[o], loc.at[3])
    gown.start()
    flc = pltpu.make_async_copy(gf.at[pl.ds(GROWS, 2)], fl_out, fl_sem)
    flc.start()
    for dy in NEAR:
        send(gf.at[pl.ds(0, GROWS)], g_out.at[o], g_s, g_r.at[dy - 1], ydev(dy))
    send(gf.at[pl.ds(0, GROWS)], g_out.at[o], gc_s, gc_r, other)

    wait_for(rb2, r2_r)
    t[2:4, mine, :] = sb2[0] + jnp.sum(rb2[...], axis=0)
    for dz in NEAR:
        send(t.at[pl.ds(2, 2), mine], t.at[pl.ds(2, 2), mine], a1m_s, a1m_r.at[dz - 1], zdev(dz))
    for dx in range(1, NX):
        send(t.at[pl.ds(2, 2), mine], t.at[pl.ds(2, 2), mine], a2m_s, a2m_r, xdev(dx))

    for dy in NEAR:
        slot = lax.rem(y + NY - dy, NY) * 2 + c
        wait_for(f_out.at[slot], f_r.at[dy - 1])
        send(f_out.at[slot], f_out.at[slot], fc_s, fc_r, other)

    for dz in NEAR:
        h = lax.rem(z + NZ - dz, NZ) * NX + x
        rows = pl.ds(pl.multiple_of(h * CH, 8), CH)
        wait_for(t.at[pl.ds(2, 2), rows], a1m_r.at[dz - 1])
        for dx in range(1, NX):
            send(t.at[pl.ds(2, 2), rows], t.at[pl.ds(2, 2), rows], a2m_s, a2m_r, xdev(dx))

    some = pl.ds(0, (NX - 1) * NZ * CH)
    wait_for(t.at[pl.ds(0, 2), some], a2e_r)
    ends_out = pltpu.make_async_copy(t.at[pl.ds(0, 2)], t_out.at[pl.ds(0, 2)], out_sem.at[0])
    ends_out.start()

    for dy in NEAR:
        slot = lax.rem(y + NY - dy, NY) * 2 + c
        wait_for(g_out.at[slot], g_r.at[dy - 1])
        send(g_out.at[slot], g_out.at[slot], gc_s, gc_r, other)

    wait_for(t.at[pl.ds(2, 2), some], a2m_r)
    mids_out = pltpu.make_async_copy(t.at[pl.ds(2, 2)], t_out.at[pl.ds(2, 2)], out_sem.at[1])
    mids_out.start()
    wait_for(f_out.at[pl.ds(0, NY)], fc_r)
    wait_for(g_out.at[pl.ds(0, NY)], gc_r)

    fown.wait()
    gown.wait()
    flc.wait()
    wait_for(f_out.at[pl.ds(0, NY - 1)], f_s)
    wait_for(f_out.at[pl.ds(0, NY)], fc_s)
    wait_for(g_out.at[pl.ds(0, NY - 1)], g_s)
    wait_for(g_out.at[pl.ds(0, NY)], gc_s)
    wait_for(grb.at[pl.ds(1, NIN - 1)], grs_s)
    wait_for(grb.at[pl.ds(1, NIN - 1)], gag_s)
    wait_for(rb1.at[:], r1_s)
    wait_for(rb2, r2_s)
    for s in (a1e_s, a1m_s):
        wait_for(t.at[pl.ds(0, 2), pl.ds(0, (NZ - 1) * CH)], s)
    for s in (a2e_s, a2m_s):
        wait_for(t.at[pl.ds(0, 2), some], s)

    @pl.when(is_root)
    def _():
        wait_for(ce.at[pl.ds(CH, (NIN - 1) * CH)], sc_s)

    ends_out.wait()
    mids_out.wait()


def split(v):
    hi = v.astype(jnp.bfloat16)
    return hi, (v - hi.astype(F32)).astype(jnp.bfloat16)


def dot3(ah, al, bh, bl):
    dot = lambda a, b: jnp.dot(a, b, preferred_element_type=F32)
    return dot(ah, bh) + (dot(ah, bl) + dot(al, bh))


def compensate(rt, bo_ref, keep_ref, fl_ref, dv_ref, t_ref, f_ref, g_ref, w_ref, o_ref, fh, flo, gh, glo, eh, elo):
    i = pl.program_id(0)
    me = lax.axis_index("in")
    blk = 2 * TILE
    bo = [bo_ref[k] for k in range(NBLK)]

    @pl.when(i == 0)
    def _():
        for k in range(NBLK):
            for lb in range(2):
                b = me * 2 + lb
                done = bo[0] == b
                for j in range(1, k + 1):
                    done = jnp.logical_or(done, bo[j] == b)
                v = f_ref[:, k, :, pl.ds(lb * blk, blk)].reshape(blk, blk)
                hi, lo = split(jnp.where(done, 0.0, v))
                fh[pl.ds(k * blk, blk), pl.ds(lb * blk, blk)] = hi
                flo[pl.ds(k * blk, blk), pl.ds(lb * blk, blk)] = lo
        for p in range(len(PAIRS)):
            for half in range(2):
                v = g_ref[:, pl.ds(p * 4 + half * 2, 2)].reshape(blk, TILE)
                hi, lo = split(v)
                gh[p, :, pl.ds(half * TILE, TILE)] = hi
                glo[p, :, pl.ds(half * TILE, TILE)] = lo

    seen = jnp.int32(0)
    for k in range(NBLK):
        is_first, is_last = bo[k] == 0, bo[k] == 2 * NIN - 1
        src = jnp.where(is_first, 0, jnp.where(is_last, 1, 2 + seen))
        seen = seen + jnp.where(jnp.logical_or(is_first, is_last), 0, 1)
        acc = None
        for j in range(k):
            p = PAIRS.index((j, k))
            part = dot3(eh[:, pl.ds(j * blk, blk)], elo[:, pl.ds(j * blk, blk)], gh[p], glo[p])
            acc = part if acc is None else acc + part
        base = jnp.int32(0)
        for tt in range(16):
            base = base + jnp.where(jnp.logical_and(tt < i * rt * 2, fl_ref[0, k, tt] > 0.5), 1, 0)
        for r in range(rt):
            for cc in range(2):
                on = fl_ref[0, k, (i * rt + r) * 2 + cc] > 0.5
                rows = pl.ds(pl.multiple_of(jnp.where(on, base, 0) * TILE, TILE), TILE)
                v = t_ref[src, rows, :] * dv_ref[1, 2 * k + cc : 2 * k + cc + 1, :]
                if acc is not None:
                    v = v - acc[r * TILE : (r + 1) * TILE, cc * TILE : (cc + 1) * TILE]
                hi, lo = split(jnp.where(on, v, 0.0))
                at = (pl.ds(r * TILE, TILE), pl.ds(k * blk + cc * TILE, TILE))
                eh[at] = hi
                elo[at] = lo
                base = base + jnp.where(on, 1, 0)

    upd = dot3(eh[...], elo[...], fh[...], flo[...])
    for cc in range(4):
        b = me * 2 + cc // 2
        done = bo[0] == b
        for j in range(1, NBLK):
            done = jnp.logical_or(done, bo[j] == b)
        for r in range(rt):
            kept = jnp.where(done, keep_ref[cc, i * rt + r], 1).astype(F32)
            at = (slice(r * TILE, (r + 1) * TILE), slice(cc * TILE, (cc + 1) * TILE))
            o_ref[at] = (w_ref[at] - upd[at]) * kept


def body(weight, keep_tiles, factor_rows, diag_inverse, block_order):
    rows, cols = weight.shape
    fshape = factor_rows.shape
    smem = pl.BlockSpec(memory_space=pltpu.SMEM)
    vmem = pl.BlockSpec(memory_space=pltpu.VMEM)
    anym = pl.BlockSpec(memory_space=pl.ANY)
    dma = pltpu.SemaphoreType.DMA
    one = dma(())
    mids, ends, shares = pl.pallas_call(
        stage,
        out_shape=(
            jax.ShapeDtypeStruct((2, ROWS, TILE), F32),
            jax.ShapeDtypeStruct((ROWS, TILE), F32),
            jax.ShapeDtypeStruct((NIN, 8, TILE), F32),
        ),
        in_specs=[smem, smem, anym, vmem, vmem],
        out_specs=(vmem, vmem, vmem),
        scratch_shapes=[pltpu.VMEM((3, rows, 2 * TILE), F32), dma((3,))],
        compiler_params=pltpu.CompilerParams(vmem_limit_bytes=12 << 20),
    )(block_order, keep_tiles.T, weight, factor_rows, diag_inverse.reshape(1, cols))
    tiles, facs, pans, flags = pl.pallas_call(
        exchange,
        out_shape=(
            jax.ShapeDtypeStruct((NBLK, ROWS, TILE), F32),
            jax.ShapeDtypeStruct((NOUT,) + fshape, F32),
            jax.ShapeDtypeStruct((NOUT, GROWS, 8, TILE), F32),
            jax.ShapeDtypeStruct((2, 8, TILE), F32),
        ),
        in_specs=[anym, anym, anym, anym],
        out_specs=(anym, anym, anym, anym),
        scratch_shapes=[
            pltpu.VMEM((NBLK, ROWS, TILE), F32),
            pltpu.VMEM((2, NZ, CH, TILE), F32),
            pltpu.VMEM((NIN, 8, TILE), F32),
            pltpu.VMEM((NZ, NX - 1, 2, CH, TILE), F32),
            pltpu.VMEM((NZ, 2, CH, TILE), F32),
            pltpu.VMEM((NZ - 1, 2, CH, TILE), F32),
            pltpu.VMEM((NIN, 8, TILE), F32),
            pltpu.VMEM((NIN, 8, TILE), F32),
            dma((5,)), one, dma((2,)),
            one, dma((NY - 1,)), one, one,
            one, dma((NY - 1,)), one, one,
            one, one, one, one,
            one, dma((2,)), one, dma((NZ,)), one, one,
            one, dma((NZ - 1,)), one, one,
            one, dma((NZ - 1,)), one, one,
        ],
        compiler_params=pltpu.CompilerParams(
            collective_id=0, has_side_effects=True, vmem_limit_bytes=16 << 20
        ),
    )(mids.reshape(2, NZ, NX * CH, TILE), ends, shares, factor_rows)

    rt = 4
    br = rt * TILE
    depth = NBLK * 2 * TILE
    return pl.pallas_call(
        lambda *refs: compensate(rt, *refs),
        grid=(rows // br,),
        out_shape=jax.ShapeDtypeStruct((rows, cols), F32),
        in_specs=[
            smem, smem, smem, vmem, vmem, vmem, vmem,
            pl.BlockSpec((br, cols), lambda i: (i, 0)),
        ],
        out_specs=pl.BlockSpec((br, cols), lambda i: (i, 0)),
        scratch_shapes=[
            pltpu.VMEM((depth, cols), jnp.bfloat16),
            pltpu.VMEM((depth, cols), jnp.bfloat16),
            pltpu.VMEM((len(PAIRS), 2 * TILE, 2 * TILE), jnp.bfloat16),
            pltpu.VMEM((len(PAIRS), 2 * TILE, 2 * TILE), jnp.bfloat16),
            pltpu.VMEM((br, depth), jnp.bfloat16),
            pltpu.VMEM((br, depth), jnp.bfloat16),
        ],
        compiler_params=pltpu.CompilerParams(vmem_limit_bytes=32 << 20),
    )(block_order, keep_tiles.T, flags, flags, tiles, facs, pans, weight)


def solution(mesh):
    return jax.shard_map(
        body,
        mesh=mesh,
        in_specs=(P("out", "in"), P("out", "in"), P(None, "out", "in"), P("in"), P()),
        out_specs=P("out", "in"),
        check_vma=False,
    )
```

time: 697 us -> 87.5 us (0.13)
  the two profiles are of different devices: /device:TPU:1 before, /device:TPU:8 now
where the time goes in v1:
time: 87.5 us; the launch traced here: 87.3 us
  Pallas kernels  82.7 us (95%)
  local copies, waits for them, and re-layouts  4.53 us (5%)
    pallas_call x1, Pallas kernels, body(): pl.pallas_call(exchange, out_shape=(jax.ShapeDtypeStruct((NBLK, ROWS, TIL...  68.1 us
    pallas_call x1, Pallas kernels, body(): pl.pallas_call(lambda *refs: compensate(rt, *refs), grid=(rows // br,), o...  13.4 us
    unnamed x18, local copies, waits for them, and re-layouts  4.53 us

profile of v1, /device:TPU:8, one launch (start us, length us, event | category | flops | bytes accessed | tf_op | source)
XLA Modules:
  0.0 87.3 jit_solution(9060945788814939908)
XLA Ops:
  0.0 0.0 copy-start
  0.0 1.6 %copy-done = f32[1024,512]{1,0:T(8,128)S(1)} copy-done((f32[1024,512]{1,0:T(8,128)S(1)}, f32[1024,512]{1,0:T(8,128)}, u32[]{:S(2)}) %copy-start) | copy-done | bytes 2097176
  1.6 0.0 copy-start.2
  1.6 0.9 %copy-done.2 = f32[4,16,512]{2,1,0:T(8,128)S(1)} copy-done((f32[4,16,512]{2,1,0:T(8,128)S(1)}, f32[4,16,512]{2,1,0:T(8,128)}, u32[]{:S(2)}) %copy-start.2) | copy-done | bytes 131096
  2.5 0.0 copy-start.4
  2.5 0.7 copy-done.4
  3.2 0.0 copy-start.6
  3.2 0.7 copy-done.6
  3.9 0.0 copy-start.7
  3.9 0.7 copy-done.7
  4.5 0.0 copy-start.3
  4.5 0.0 copy-start.1
  4.5 0.0 copy-start.5
  4.5 0.0 copy-start.8
  4.5 1.2 %shard_map.55 = (f32[2,1280,128]{2,1,0:T(8,128)S(1)}, f32[1280,128]{1,0:T(8,128)S(1)}, f32[32,8,128]{2,1,0:T(8,128)S(1)}) custom-call(s32[4]{0:T(128)S(1)} %copy-done.7, s32[4,8]{1,0:T(4,128)S(1)} %bitcast.4, f32[1024,512]{1,0:T(8,128)S(1)} %copy-done, f32[4,16,512]{2,1,0:T(8,128)S(1)} %copy-done.2, f32[1,512]{1,0:T(1,128)S(1)} %bitcast.6), custom_call_target="tpu_custom_call" | custom-call | tf_op jit(solution)/shard_map/pallas_call | solution.py:385
  5.7 0.0 copy-done.3
  5.7 68.1 %shard_map.56 = (f32[4,1280,128]{2,1,0:T(8,128)S(1)}, f32[16,4,16,512]{3,2,1,0:T(8,128)S(1)}, f32[16,24,8,128]{3,2,1,0:T(8,128)S(1)}, f32[2,8,128]{2,1,0:T(8,128)S(1)}) custom-call(f32[2,8,160,128]{3,2,1,0:T(8,128)S(1)} %bitcast.3, f32[1280,128]{1,0:T(8,128)S(1)} %get-tuple-element.13.ce, f32[32,8,128]{2,1,0:T(8,128)S(1)} %get-tuple-element.14.gc_hbm, ...), custom_call_target="tpu_custom_call" | custom-call | tf_op jit(solution)/shard_map/pallas_call | solution.py:397
  73.9 0.0 copy-done.1
  73.9 0.0 copy-done.5
  73.9 0.0 copy-done.8
  73.9 13.4 %shard_map.57 = f32[1024,512]{1,0:T(8,128)} custom-call(s32[4]{0:T(128)S(1)} %copy-done.8, s32[4,8]{1,0:T(4,128)S(1)} %bitcast.5, f32[2,8,128]{2,1,0:T(8,128)S(1)} %get-tuple-element.15.refs_2_.refs_3_, f32[2,8,128]{2,1,0:T(8,128)S(1)} %get-tuple-element.15.refs_2_.refs_3_, f32[4,1280,128]{2,1,0:T(8,128)S(1)} %get-tuple-element.16.refs_4_, ...), custom_call_target="tpu_custom_call" | custom-call | tf_op jit(solution)/shard_map/pallas_call | solution.py:432
Async XLA Ops:
  0.0 1.6 %copy-start = (f32[1024,512]{1,0:T(8,128)S(1)}, f32[1024,512]{1,0:T(8,128)}, u32[]{:S(2)}) copy-start(f32[1024,512]{1,0:T(8,128)} %refs_7_.1) | copy-start | bytes 6291460
  1.6 0.9 %copy-start.2 = (f32[4,16,512]{2,1,0:T(8,128)S(1)}, f32[4,16,512]{2,1,0:T(8,128)}, u32[]{:S(2)}) copy-start(f32[4,16,512]{2,1,0:T(8,128)} %f_hbm.1) | copy-start | bytes 393220
  2.5 0.7 copy-start.4
  3.2 0.7 copy-start.6
  3.9 0.7 copy-start.7
  4.5 1.2 %copy-start.3 = (f32[4,16,512]{2,1,0:T(8,128)S(1)}, f32[4,16,512]{2,1,0:T(8,128)}, u32[]{:S(2)}) copy-start(f32[4,16,512]{2,1,0:T(8,128)} %f_hbm.1) | copy-start | bytes 393220
  4.5 69.4 %copy-start.1 = (f32[1024,512]{1,0:T(8,128)S(1)}, f32[1024,512]{1,0:T(8,128)}, u32[]{:S(2)}) copy-start(f32[1024,512]{1,0:T(8,128)} %refs_7_.1) | copy-start | bytes 6291460
  4.5 69.4 %copy-start.5 = (s32[8,4]{0,1:T(4,128)S(1)}, s32[8,4]{0,1:T(4,128)}, u32[]{:S(2)}) copy-start(s32[8,4]{0,1:T(4,128)} %param.6) | copy-start | bytes 388
  4.5 69.4 %copy-start.8 = (s32[4]{0:T(128)S(1)}, s32[4]{0:T(128)}, u32[]{:S(2)}) copy-start(s32[4]{0:T(128)} %refs_0_.1) | copy-start | bytes 52

commit v2 on v1

v2 whole, which is shorter than its diff:
```python
import jax
import jax.numpy as jnp
from jax import lax
from jax.experimental import pallas as pl
from jax.experimental.pallas import tpu as pltpu
from jax.sharding import PartitionSpec as P

MESH = pl.DeviceIdType.MESH
TILE = 128
NBLK = 4
MAXP = 10
NZ, NX, NY = 8, 4, 8
NIN, NOUT = NZ * NX, NY * 2
ROWS = MAXP * TILE
CH = ROWS // NIN
PAIRS = [(j, k) for k in range(NBLK) for j in range(k)]
GROWS = len(PAIRS) * 4
F32 = jnp.float32
NEAR = (1, 7, 2, 6, 3, 5, 4)
FAR = (4, 3, 5, 2, 6, 1, 7)


def wait_for(ref, sem):
    pltpu.make_async_copy(ref, ref, sem).wait()


def stage(bo_hbm, keep_hbm, w_hbm, f_hbm, d_hbm, m_out, ce_out, gc_ref, bo_ref, keep_ref, w, f_ref, d_ref, sem):
    moves = [
        pltpu.make_async_copy(src, dst, sem.at[i])
        for i, (src, dst) in enumerate(
            ((bo_hbm, bo_ref), (keep_hbm, keep_ref), (d_hbm, d_ref), (f_hbm, f_ref), (w_hbm, w))
        )
    ]
    for move in moves:
        move.start()
    me = lax.axis_index("in")
    last = NIN - 1
    blk = 2 * TILE
    m_out[...] = jnp.zeros_like(m_out)
    gc_ref[...] = jnp.zeros_like(gc_ref)
    for move in moves[:4]:
        move.wait()
    first_b, last_b = 0, 2 * NIN - 1
    bo = [bo_ref[k] for k in range(NBLK)]
    mid = [jnp.int32(0), jnp.int32(0)]
    seen = jnp.int32(0)
    for k in range(NBLK):
        is_mid = jnp.logical_and(bo[k] != first_b, bo[k] != last_b)
        for q in range(2):
            mid[q] = jnp.where(jnp.logical_and(is_mid, seen == q), bo[k], mid[q])
        seen = seen + is_mid.astype(jnp.int32)
    is_root = jnp.logical_or(me == 0, me == last)
    jobs = [
        (mid[0] // 2 == me, mid[0] % 2, m_out.at[0]),
        (mid[1] // 2 == me, mid[1] % 2, m_out.at[1]),
        (is_root, jnp.where(me == last, 1, 0), ce_out),
    ]

    row = lax.broadcasted_iota(jnp.int32, (8, TILE), 0)
    lane = lax.broadcasted_iota(jnp.int32, (8, TILE), 1)
    for k in range(NBLK):
        own = bo[k] // 2 == me

        @pl.when(own)
        def _():
            off = pl.multiple_of((bo[k] % 2) * blk, blk)
            cb = (bo[k] % 2) * 2
            flags = jnp.zeros((8, TILE), F32)
            for tt in range(16):
                pr = (1 - keep_ref[cb + tt % 2, tt // 2]).astype(F32)
                flags = jnp.where(jnp.logical_and(row == k, lane == tt), pr, flags)
            gc_ref[GROWS] = gc_ref[GROWS] + flags
            for half in range(2):
                d = d_ref[0:1, pl.ds(pl.multiple_of(off + half * TILE, TILE), TILE)]
                gc_ref[GROWS + 1, pl.ds(2 * k + half, 1), :] = d

        for p, (j, kk) in enumerate(PAIRS):
            if kk != k:
                continue

            @pl.when(own)
            def _():
                for half in range(2):
                    cols = pl.ds(pl.multiple_of((bo[k] % 2) * blk + half * TILE, TILE), TILE)
                    d = d_ref[0:1, cols]
                    for rh in range(2):
                        gc_ref[p * 4 + half * 2 + rh] = f_ref[j, pl.ds(rh * 8, 8), cols] * d

    moves[4].wait()
    for i, (own, lb, out) in enumerate(jobs):

        @pl.when(own)
        def _():
            if i == 2:
                out[...] = jnp.zeros((ROWS, TILE), F32)
            base = pl.multiple_of(lb * blk, blk)
            cnt = jnp.int32(0)
            for tt in range(16):
                r, cc = tt // 2, tt % 2
                pr = 1 - keep_ref[lb * 2 + cc, r]

                @pl.when(pr == 1)
                def _():
                    rows = pl.ds(pl.multiple_of(cnt * TILE, TILE), TILE)
                    out[rows, :] = w[pl.ds(r * TILE, TILE), pl.ds(base + cc * TILE, TILE)]

                cnt = jnp.minimum(cnt + pr, MAXP - 1 if tt == 15 else MAXP)


def exchange(m, ce, gc_hbm, f_hbm, t_out, f_out, g_out, fl_out,
             om, mq, gc, rb1, sb2, rb2, grb, gf,
             loc, fl_sem, f_s, f_r, fc_s, fc_r, g_s, g_r, gc_s, gc_r, grs_s, grs_r, gag_s, gag_r,
             sc_s, sc_r, r1_s, r1_r, r2_s, r2_r, a1_s, a1_r, a2_s, a2_r, ex_s, ex_r, z_s, zp_r, zm_r, zl_r):
    o = lax.axis_index("out")
    me = lax.axis_index("in")
    y, c = o // 2, o % 2
    z, x = me // NX, me % NX
    last = NIN - 1
    is_root = jnp.logical_or(me == 0, me == last)

    gcopy = pltpu.make_async_copy(gc_hbm, gc, loc.at[0])
    gcopy.start()
    mcopy = pltpu.make_async_copy(m.at[:, :, pl.ds(pl.multiple_of(x * CH, 8), CH)], mq, loc.at[1])
    mcopy.start()
    fown = pltpu.make_async_copy(f_hbm, f_out.at[o], loc.at[2])
    fown.start()

    def ydev(dy):
        return (lax.rem(y + dy, NY) * 2 + c, me)

    def zdev(dz):
        return (o, lax.rem(z + dz, NZ) * NX + x)

    def xdev(dx):
        return (o, z * NX + lax.rem(x + dx, NX))

    other = (y * 2 + 1 - c, me)

    def send(src, dst, ssem, rsem, dev):
        pltpu.make_async_remote_copy(
            src_ref=src, dst_ref=dst, send_sem=ssem, recv_sem=rsem, device_id=dev, device_id_type=MESH
        ).start()

    barrier = pltpu.get_barrier_semaphore()

    def greet(r, _):
        pl.semaphore_signal(barrier, inc=1, device_id=(o, lax.rem(me + r, NIN)), device_id_type=MESH)
        return 0

    lax.fori_loop(1, NIN, greet, 0)
    for dy in range(1, NY):
        pl.semaphore_signal(barrier, inc=1, device_id=ydev(dy), device_id_type=MESH)
    pl.semaphore_signal(barrier, inc=1, device_id=other, device_id_type=MESH)
    pl.semaphore_wait(barrier, NIN - 1 + NY - 1 + 1)

    gcopy.wait()

    def spread_g(r, _):
        peer = lax.rem(me + r, NIN)
        send(gc.at[peer], grb.at[r], grs_s, grs_r, (o, peer))
        return 0

    lax.fori_loop(1, NIN, spread_g, 0)

    for dz in FAR + (0,):
        for dx in range(1, NX):
            part = pl.ds(pl.multiple_of(lax.rem(x + dx, NX) * CH, 8), CH)
            send(m.at[:, lax.rem(z + dz, NZ), part], rb1.at[dz, dx - 1], r1_s, r1_r.at[dz], xdev(dx))

    for e in range(2):
        root = e * last

        @pl.when(me == root)
        def _():
            def scatter(r, _):
                peer = lax.rem(me + r, NIN)
                rows = pl.ds(pl.multiple_of(peer * CH, 8), CH)
                send(ce.at[rows], t_out.at[e, rows], sc_s, sc_r.at[e], (o, peer))
                return 0

            lax.fori_loop(1, NIN, scatter, 0)

    def yslot(dst, dy):
        return dst.at[lax.rem(y + NY - dy, NY) * 2 + c]

    def y_start(src, dst, ssem, rsem, csem, crsem):
        for dy in (1, NY - 1, 2, NY - 2):
            send(src, dst.at[o], ssem, rsem.at[dy - 1], ydev(dy))
        send(src, dst.at[o], csem, crsem, other)

    def y_onward(dst, ssem, rsem, csem, crsem):
        for dy, hops in ((2, ((1, 3), (2, 4))), (NY - 2, ((NY - 1, NY - 3),))):
            src = yslot(dst, dy)
            wait_for(src, rsem.at[dy - 1])
            for hop, total in hops:
                send(src, src, ssem, rsem.at[total - 1], ydev(hop))
            send(src, src, csem, crsem, other)

    def y_finish(dst, rsem, csem, crsem):
        for dy in (1, NY - 1, 3, NY - 3, 4):
            src = yslot(dst, dy)
            wait_for(src, rsem.at[dy - 1])
            send(src, src, csem, crsem, other)

    y_start(f_hbm, f_out, f_s, f_r, fc_s, fc_r)

    def chunk(dz, dx):
        h = lax.rem(z + NZ - dz, NZ) * NX + lax.rem(x + NX - dx, NX)
        return pl.ds(pl.multiple_of(h * CH, 8), CH)

    mine = chunk(0, 0)

    pair = pl.ds(2, 2)

    def from_z(dz, src):
        dst = t_out.at[pair, chunk(dz, 0)]
        for dx in range(1, NX):
            send(src, dst, a2_s, a2_r, xdev(dx))

    def zrow(dz, e=pl.ds(0, 2)):
        return t_out.at[e, pl.ds(pl.multiple_of(lax.rem(z + NZ - dz, NZ) * NX * CH, 8), NX * CH)]

    def round_z(n):
        if n:
            wait_for(zrow(n), zp_r.at[n - 1])
            wait_for(zrow(NZ - n), zm_r.at[n - 1])
        if n < NZ // 2 - 1:
            send(zrow(n), zrow(n), z_s, zp_r.at[n], zdev(1))
            send(zrow(NZ - n), zrow(NZ - n), z_s, zm_r.at[n], zdev(NZ - 1))
        else:
            send(zrow(n, 0), zrow(n, 0), z_s, zl_r.at[0], zdev(1))
            send(zrow(NZ - n, 1), zrow(NZ - n, 1), z_s, zl_r.at[1], zdev(NZ - 1))

    wait_for(grb.at[pl.ds(1, NIN - 1)], grs_r)
    grb[0] = gc[me]
    gf[me] = jnp.sum(grb[...], axis=0)

    def back_g(r, _):
        send(gf.at[me], gf.at[me], gag_s, gag_r, (o, lax.rem(me + r, NIN)))
        return 0

    lax.fori_loop(1, NIN, back_g, 0)

    for e in range(2):
        root = e * last

        @pl.when(me == root)
        def _():
            own = pltpu.make_async_copy(ce.at[mine], t_out.at[e, mine], loc.at[4])
            own.start()
            own.wait()

        @pl.when(me != root)
        def _():
            wait_for(t_out.at[e, mine], sc_r.at[e])

    for dx in range(1, NX):
        send(t_out.at[pl.ds(0, 2), mine], t_out.at[pl.ds(0, 2), mine], ex_s, ex_r, xdev(dx))

    mcopy.wait()
    y_onward(f_out, f_s, f_r, fc_s, fc_r)

    for dz in FAR + (0,):
        wait_for(rb1.at[dz], r1_r.at[dz])
        acc = mq[:, lax.rem(z + dz, NZ)]
        for q in range(NX - 1):
            acc = acc + rb1[dz, q]
        sb2[dz] = acc
        if dz:
            send(sb2.at[dz], rb2.at[dz - 1], r2_s, r2_r, zdev(dz))

    wait_for(t_out.at[pl.ds(0, 2), pl.ds(0, (NX - 1) * CH)], ex_r)
    round_z(0)

    wait_for(gf.at[pl.ds(1, NIN - 1)], gag_r)
    gown = pltpu.make_async_copy(gf.at[pl.ds(0, GROWS)], g_out.at[o], loc.at[3])
    gown.start()
    flc = pltpu.make_async_copy(gf.at[pl.ds(GROWS, 2)], fl_out, fl_sem)
    flc.start()
    y_start(gf.at[pl.ds(0, GROWS)], g_out, g_s, g_r, gc_s, gc_r)

    wait_for(rb2, r2_r)
    om[...] = sb2[0] + jnp.sum(rb2[...], axis=0)
    for dz in FAR:
        send(om, t_out.at[pair, mine], a1_s, a1_r.at[dz - 1], zdev(dz))
    from_z(0, om)
    omc = pltpu.make_async_copy(om, t_out.at[pair, mine], loc.at[5])
    omc.start()
    round_z(1)
    y_finish(f_out, f_r, fc_s, fc_r)
    for n, dz in enumerate(NEAR):
        wait_for(t_out.at[pair, chunk(dz, 0)], a1_r.at[dz - 1])
        from_z(dz, t_out.at[pair, chunk(dz, 0)])
        if n == 2:
            round_z(2)
    y_onward(g_out, g_s, g_r, gc_s, gc_r)
    round_z(3)
    y_finish(g_out, g_r, gc_s, gc_r)

    wait_for(zrow(4, 0), zl_r.at[0])
    wait_for(zrow(4, 1), zl_r.at[1])
    wait_for(t_out.at[pair, pl.ds(0, 3 * NZ * CH)], a2_r)
    wait_for(f_out.at[pl.ds(0, NY)], fc_r)
    wait_for(g_out.at[pl.ds(0, NY)], gc_r)
    omc.wait()
    fown.wait()
    gown.wait()
    flc.wait()
    wait_for(f_out.at[pl.ds(0, NY - 1)], f_s)
    wait_for(f_out.at[pl.ds(0, NY)], fc_s)
    wait_for(g_out.at[pl.ds(0, NY - 1)], g_s)
    wait_for(g_out.at[pl.ds(0, NY)], gc_s)
    wait_for(grb.at[pl.ds(1, NIN - 1)], grs_s)
    wait_for(grb.at[pl.ds(1, NIN - 1)], gag_s)
    wait_for(rb1.at[:], r1_s)
    wait_for(rb2, r2_s)
    wait_for(t_out.at[pair, pl.ds(0, (NZ - 1) * CH)], a1_s)
    wait_for(t_out.at[pair, pl.ds(0, 3 * NZ * CH)], a2_s)
    wait_for(t_out.at[pl.ds(0, 2), pl.ds(0, (NX - 1) * CH)], ex_s)
    wait_for(t_out.at[pl.ds(0, 2), pl.ds(0, (NZ - 1) * NX * CH)], z_s)

    @pl.when(is_root)
    def _():
        wait_for(ce.at[pl.ds(CH, (NIN - 1) * CH)], sc_s)


def split(v):
    hi = v.astype(jnp.bfloat16)
    return hi, (v - hi.astype(F32)).astype(jnp.bfloat16)


def dot(a, b):
    return jnp.dot(a, b, preferred_element_type=F32)


def compensate(rt, bo_ref, keep_ref, fl_ref, dv_ref, t_ref, f_ref, g_ref, w_ref, o_hbm, f3, g3, e3, ob, start, osem):
    me = lax.axis_index("in")
    blk = 2 * TILE
    bo = [bo_ref[k] for k in range(NBLK)]

    for k in range(NBLK):
        for lb in range(2):
            b = me * 2 + lb
            done = bo[0] == b
            for j in range(1, k + 1):
                done = jnp.logical_or(done, bo[j] == b)
            v = f_ref[:, k, :, pl.ds(lb * blk, blk)].reshape(blk, blk)
            hi, lo = split(jnp.where(done, 0.0, v))
            for n, part in enumerate((hi, hi, lo)):
                f3[pl.ds((3 * k + n) * blk, blk), pl.ds(lb * blk, blk)] = part
    for p, (j, k) in enumerate(PAIRS):
        for half in range(2):
            v = g_ref[:, pl.ds(p * 4 + half * 2, 2)].reshape(blk, TILE)
            hi, lo = split(v)
            for n, part in enumerate((hi, hi, lo)):
                g3[k - 1, pl.ds((3 * j + n) * blk, blk), pl.ds(half * TILE, TILE)] = part

    srcs = []
    seen = jnp.int32(0)
    for k in range(NBLK):
        is_first, is_last = bo[k] == 0, bo[k] == 2 * NIN - 1
        srcs.append(jnp.where(is_first, 0, jnp.where(is_last, 1, 2 + seen)))
        seen = seen + jnp.where(jnp.logical_or(is_first, is_last), 0, 1)
        base = jnp.int32(0)
        for tt in range(16):
            on = fl_ref[0, k, tt] > 0.5
            start[k, tt] = jnp.where(on, base, -1)
            base = base + jnp.where(on, TILE, 0)

    nb = w_ref.shape[0] // (rt * TILE)
    br = rt * TILE
    for k in range(NBLK):
        for i in range(nb):
            acc = dot(e3[pl.ds(i * br, br), : 3 * k * blk], g3[k - 1, : 3 * k * blk]) if k else None
            for r in range(rt):
                for cc in range(2):
                    base = start[k, (i * rt + r) * 2 + cc]
                    rows = pl.ds(pl.multiple_of(jnp.maximum(base, 0), TILE), TILE)
                    v = t_ref[srcs[k], rows, :] * dv_ref[1, 2 * k + cc : 2 * k + cc + 1, :]
                    if acc is not None:
                        v = v - acc[r * TILE : (r + 1) * TILE, cc * TILE : (cc + 1) * TILE]
                    hi, lo = split(jnp.where(base >= 0, v, 0.0))
                    for n, part in enumerate((hi, lo, hi)):
                        e3[pl.ds(i * br + r * TILE, TILE), pl.ds((3 * k + n) * blk + cc * TILE, TILE)] = part

    copies = []
    for i in range(nb):
        upd = dot(e3[pl.ds(i * br, br), :], f3[...])
        for cc in range(4):
            b = me * 2 + cc // 2
            done = bo[0] == b
            for j in range(1, NBLK):
                done = jnp.logical_or(done, bo[j] == b)
            for r in range(rt):
                kept = jnp.where(done, keep_ref[cc, i * rt + r], 1).astype(F32)
                at = (pl.ds(i * br + r * TILE, TILE), pl.ds(cc * TILE, TILE))
                ob[at] = (w_ref[at] - upd[r * TILE : (r + 1) * TILE, cc * TILE : (cc + 1) * TILE]) * kept
        rows = pl.ds(i * br, br)
        copies.append(pltpu.make_async_copy(ob.at[rows], o_hbm.at[rows], osem.at[i]))
        copies[-1].start()
    for copy in copies:
        copy.wait()


def body(weight, keep_tiles, factor_rows, diag_inverse, block_order):
    rows, cols = weight.shape
    fshape = factor_rows.shape
    smem = pl.BlockSpec(memory_space=pltpu.SMEM)
    vmem = pl.BlockSpec(memory_space=pltpu.VMEM)
    anym = pl.BlockSpec(memory_space=pl.ANY)
    hbm = pl.BlockSpec(memory_space=pltpu.HBM)
    dma = pltpu.SemaphoreType.DMA
    one = dma(())
    mids, ends, shares = pl.pallas_call(
        stage,
        out_shape=(
            jax.ShapeDtypeStruct((2, ROWS, TILE), F32),
            jax.ShapeDtypeStruct((ROWS, TILE), F32),
            jax.ShapeDtypeStruct((NIN, 8, TILE), F32),
        ),
        in_specs=[hbm] * 5,
        out_specs=(vmem, vmem, vmem),
        scratch_shapes=[
            pltpu.SMEM(block_order.shape, jnp.int32),
            pltpu.SMEM(keep_tiles.T.shape, jnp.int32),
            pltpu.VMEM((rows, cols), F32),
            pltpu.VMEM(fshape, F32),
            pltpu.VMEM((1, cols), F32),
            dma((5,)),
        ],
        compiler_params=pltpu.CompilerParams(vmem_limit_bytes=12 << 20),
    )(block_order, keep_tiles.T, weight, factor_rows, diag_inverse.reshape(1, cols))
    tiles, facs, pans, flags = pl.pallas_call(
        exchange,
        out_shape=(
            jax.ShapeDtypeStruct((NBLK, ROWS, TILE), F32),
            jax.ShapeDtypeStruct((NOUT,) + fshape, F32),
            jax.ShapeDtypeStruct((NOUT, GROWS, 8, TILE), F32),
            jax.ShapeDtypeStruct((2, 8, TILE), F32),
        ),
        in_specs=[anym, anym, anym, anym],
        out_specs=(anym, anym, anym, anym),
        scratch_shapes=[
            pltpu.VMEM((2, CH, TILE), F32),
            pltpu.VMEM((2, NZ, CH, TILE), F32),
            pltpu.VMEM((NIN, 8, TILE), F32),
            pltpu.VMEM((NZ, NX - 1, 2, CH, TILE), F32),
            pltpu.VMEM((NZ, 2, CH, TILE), F32),
            pltpu.VMEM((NZ - 1, 2, CH, TILE), F32),
            pltpu.VMEM((NIN, 8, TILE), F32),
            pltpu.VMEM((NIN, 8, TILE), F32),
            dma((6,)), one,
            one, dma((NY - 1,)), one, one,
            one, dma((NY - 1,)), one, one,
            one, one, one, one,
            one, dma((2,)), one, dma((NZ,)), one, one,
            one, dma((NZ - 1,)), one, one, one, one, one, dma((3,)), dma((3,)), dma((2,)),
        ],
        compiler_params=pltpu.CompilerParams(
            collective_id=0, has_side_effects=True, vmem_limit_bytes=16 << 20
        ),
    )(mids.reshape(2, NZ, NX * CH, TILE), ends, shares, factor_rows)

    rt = 4
    br = rt * TILE
    depth = NBLK * 2 * TILE
    bf16 = jnp.bfloat16
    return pl.pallas_call(
        lambda *refs: compensate(rt, *refs),
        out_shape=jax.ShapeDtypeStruct((rows, cols), F32),
        in_specs=[smem, smem, smem, vmem, vmem, vmem, vmem, vmem],
        out_specs=anym,
        scratch_shapes=[
            pltpu.VMEM((3 * depth, cols), bf16),
            pltpu.VMEM((NBLK - 1, 3 * (NBLK - 1) * 2 * TILE, 2 * TILE), bf16),
            pltpu.VMEM((rows, 3 * depth), bf16),
            pltpu.VMEM((rows, cols), F32),
            pltpu.SMEM((NBLK, 16), jnp.int32),
            dma((rows // br,)),
        ],
        compiler_params=pltpu.CompilerParams(vmem_limit_bytes=24 << 20),
    )(block_order, keep_tiles.T, flags, flags, tiles, facs, pans, weight)


def solution(mesh):
    return jax.shard_map(
        body,
        mesh=mesh,
        in_specs=(P("out", "in"), P("out", "in"), P(None, "out", "in"), P("in"), P()),
        out_specs=P("out", "in"),
        check_vma=False,
    )
```

time: 87.5 us -> 79 us (0.903)
  the two profiles are of different devices: /device:TPU:8 before, /device:TPU:1 now
where the time goes in v2:
time: 79 us; the launch traced here: 77.7 us
  Pallas kernels  73.1 us (93%)
  local copies, waits for them, and re-layouts  4.53 us (6%)
    pallas_call x1, Pallas kernels, body(): pl.pallas_call(exchange, out_shape=(jax.ShapeDtypeStruct((NBLK, ROWS, TIL...  63.8 us
    pallas_call x1, Pallas kernels, body(): pl.pallas_call(lambda *refs: compensate(rt, *refs), out_shape=jax.ShapeDt...  8.3 us
    unnamed x18, local copies, waits for them, and re-layouts  4.53 us

profile of v2, /device:TPU:1, one launch (start us, length us, event | category | flops | bytes accessed | tf_op | source)
XLA Modules:
  0.0 77.7 jit_solution(15953639730401758840)
XLA Ops:
  0.0 0.0 copy-start
  0.0 1.6 %copy-done = f32[1024,512]{1,0:T(8,128)S(1)} copy-done((f32[1024,512]{1,0:T(8,128)S(1)}, f32[1024,512]{1,0:T(8,128)}, u32[]{:S(2)}) %copy-start) | copy-done | bytes 2097176
  1.6 0.0 copy-start.2
  1.6 0.9 %copy-done.2 = f32[4,16,512]{2,1,0:T(8,128)S(1)} copy-done((f32[4,16,512]{2,1,0:T(8,128)S(1)}, f32[4,16,512]{2,1,0:T(8,128)}, u32[]{:S(2)}) %copy-start.2) | copy-done | bytes 131096
  2.5 0.0 copy-start.4
  2.5 0.7 copy-done.4
  3.2 0.0 copy-start.6
  3.2 0.7 copy-done.6
  3.9 0.0 copy-start.7
  3.9 0.7 copy-done.7
  4.5 0.0 copy-start.3
  4.5 0.0 copy-start.1
  4.5 0.0 copy-start.5
  4.5 0.0 copy-start.8
  4.5 1.0 %shard_map.55 = (f32[2,1280,128]{2,1,0:T(8,128)S(1)}, f32[1280,128]{1,0:T(8,128)S(1)}, f32[32,8,128]{2,1,0:T(8,128)S(1)}) custom-call(s32[4]{0:T(128)S(1)} %copy-done.7, s32[4,8]{1,0:T(4,128)S(1)} %bitcast.4, f32[1024,512]{1,0:T(8,128)S(1)} %copy-done, f32[4,16,512]{2,1,0:T(8,128)S(1)} %copy-done.2, f32[1,512]{1,0:T(1,128)S(1)} %bitcast.6), custom_call_target="tpu_custom_call" | custom-call | tf_op jit(solution)/shard_map/pallas_call | solution.py:414
  5.5 0.0 copy-done.3
  5.5 63.8 %shard_map.56 = (f32[4,1280,128]{2,1,0:T(8,128)S(1)}, f32[16,4,16,512]{3,2,1,0:T(8,128)S(1)}, f32[16,24,8,128]{3,2,1,0:T(8,128)S(1)}, f32[2,8,128]{2,1,0:T(8,128)S(1)}) custom-call(f32[2,8,160,128]{3,2,1,0:T(8,128)S(1)} %bitcast.3, f32[1280,128]{1,0:T(8,128)S(1)} %get-tuple-element.13.ce, f32[32,8,128]{2,1,0:T(8,128)S(1)} %get-tuple-element.14.gc_hbm, ...), custom_call_target="tpu_custom_call" | custom-call | tf_op jit(solution)/shard_map/pallas_call | solution.py:433
  69.4 0.0 copy-done.1
  69.4 0.0 copy-done.5
  69.4 0.0 copy-done.8
  69.4 8.3 %shard_map.57 = f32[1024,512]{1,0:T(8,128)} custom-call(s32[4]{0:T(128)S(1)} %copy-done.8, s32[4,8]{1,0:T(4,128)S(1)} %bitcast.5, f32[2,8,128]{2,1,0:T(8,128)S(1)} %get-tuple-element.15.refs_2_.refs_3_, f32[2,8,128]{2,1,0:T(8,128)S(1)} %get-tuple-element.15.refs_2_.refs_3_, f32[4,1280,128]{2,1,0:T(8,128)S(1)} %get-tuple-element.16.refs_4_, ...), custom_call_target="tpu_custom_call" | custom-call | tf_op jit(solution)/shard_map/pallas_call | solution.py:468
Async XLA Ops:
  0.0 1.6 %copy-start = (f32[1024,512]{1,0:T(8,128)S(1)}, f32[1024,512]{1,0:T(8,128)}, u32[]{:S(2)}) copy-start(f32[1024,512]{1,0:T(8,128)} %refs_7_.1) | copy-start | bytes 6291460
  1.6 0.9 %copy-start.2 = (f32[4,16,512]{2,1,0:T(8,128)S(1)}, f32[4,16,512]{2,1,0:T(8,128)}, u32[]{:S(2)}) copy-start(f32[4,16,512]{2,1,0:T(8,128)} %f_hbm.3) | copy-start | bytes 393220
  2.5 0.7 copy-start.4
  3.2 0.7 copy-start.6
  3.9 0.7 copy-start.7
  4.5 1.0 %copy-start.3 = (f32[4,16,512]{2,1,0:T(8,128)S(1)}, f32[4,16,512]{2,1,0:T(8,128)}, u32[]{:S(2)}) copy-start(f32[4,16,512]{2,1,0:T(8,128)} %f_hbm.3) | copy-start | bytes 393220
  4.5 64.8 %copy-start.1 = (f32[1024,512]{1,0:T(8,128)S(1)}, f32[1024,512]{1,0:T(8,128)}, u32[]{:S(2)}) copy-start(f32[1024,512]{1,0:T(8,128)} %refs_7_.1) | copy-start | bytes 6291460
  4.5 64.8 %copy-start.5 = (s32[8,4]{0,1:T(4,128)S(1)}, s32[8,4]{0,1:T(4,128)}, u32[]{:S(2)}) copy-start(s32[8,4]{0,1:T(4,128)} %param.6) | copy-start | bytes 388
  4.5 64.9 %copy-start.8 = (s32[4]{0:T(128)S(1)}, s32[4]{0:T(128)}, u32[]{:S(2)}) copy-start(s32[4]{0:T(128)} %refs_0_.1) | copy-start | bytes 52

commit v3 on v2

--- a/solution.py
+++ b/solution.py
@@ -153,20 +153,6 @@
     pl.semaphore_signal(barrier, inc=1, device_id=other, device_id_type=MESH)
     pl.semaphore_wait(barrier, NIN - 1 + NY - 1 + 1)
 
-    gcopy.wait()
-
-    def spread_g(r, _):
-        peer = lax.rem(me + r, NIN)
-        send(gc.at[peer], grb.at[r], grs_s, grs_r, (o, peer))
-        return 0
-
-    lax.fori_loop(1, NIN, spread_g, 0)
-
-    for dz in FAR + (0,):
-        for dx in range(1, NX):
-            part = pl.ds(pl.multiple_of(lax.rem(x + dx, NX) * CH, 8), CH)
-            send(m.at[:, lax.rem(z + dz, NZ), part], rb1.at[dz, dx - 1], r1_s, r1_r.at[dz], xdev(dx))
-
     for e in range(2):
         root = e * last
 
@@ -179,6 +165,20 @@
                 return 0
 
             lax.fori_loop(1, NIN, scatter, 0)
+
+    gcopy.wait()
+
+    def spread_g(r, _):
+        peer = lax.rem(me + r, NIN)
+        send(gc.at[peer], grb.at[r], grs_s, grs_r, (o, peer))
+        return 0
+
+    lax.fori_loop(1, NIN, spread_g, 0)
+
+    for dz in FAR + (0,):
+        for dx in range(1, NX):
+            part = pl.ds(pl.multiple_of(lax.rem(x + dx, NX) * CH, 8), CH)
+            send(m.at[:, lax.rem(z + dz, NZ), part], rb1.at[dz, dx - 1], r1_s, r1_r.at[dz], xdev(dx))
 
     def yslot(dst, dy):
         return dst.at[lax.rem(y + NY - dy, NY) * 2 + c]
@@ -281,7 +281,7 @@
 
     wait_for(rb2, r2_r)
     om[...] = sb2[0] + jnp.sum(rb2[...], axis=0)
-    for dz in FAR:
+    for dz in NEAR:
         send(om, t_out.at[pair, mine], a1_s, a1_r.at[dz - 1], zdev(dz))
     from_z(0, om)
     omc = pltpu.make_async_copy(om, t_out.at[pair, mine], loc.at[5])

time: 79 us -> 76.9 us (0.973); the launches traced: 77.7 us -> 76.7 us
  Pallas kernels: 73.1 us -> 72.1 us
    pallas_call x1, Pallas kernels: 63.8 us -> 62.9 us  [body(): pl.pallas_call(exchange, out_shape=(jax.ShapeDtypeStruct((NBLK, ROWS, TIL...]
where the time goes in v3:
time: 76.9 us; the launch traced here: 76.7 us
  Pallas kernels  72.1 us (94%)
  local copies, waits for them, and re-layouts  4.53 us (6%)
    pallas_call x1, Pallas kernels, body(): pl.pallas_call(exchange, out_shape=(jax.ShapeDtypeStruct((NBLK, ROWS, TIL...  62.9 us
    pallas_call x1, Pallas kernels, body(): pl.pallas_call(lambda *refs: compensate(rt, *refs), out_shape=jax.ShapeDt...  8.3 us
    unnamed x18, local copies, waits for them, and re-layouts  4.53 us

profile of v3, /device:TPU:1, one launch (start us, length us, event | category | flops | bytes accessed | tf_op | source)
XLA Modules:
  0.0 76.7 jit_solution(490314498056535778)
XLA Ops:
  0.0 0.0 copy-start
  0.0 1.6 %copy-done = f32[1024,512]{1,0:T(8,128)S(1)} copy-done((f32[1024,512]{1,0:T(8,128)S(1)}, f32[1024,512]{1,0:T(8,128)}, u32[]{:S(2)}) %copy-start) | copy-done | bytes 2097176
  1.6 0.0 copy-start.2
  1.6 0.9 %copy-done.2 = f32[4,16,512]{2,1,0:T(8,128)S(1)} copy-done((f32[4,16,512]{2,1,0:T(8,128)S(1)}, f32[4,16,512]{2,1,0:T(8,128)}, u32[]{:S(2)}) %copy-start.2) | copy-done | bytes 131096
  2.5 0.0 copy-start.4
  2.5 0.7 copy-done.4
  3.2 0.0 copy-start.6
  3.2 0.7 copy-done.6
  3.9 0.0 copy-start.7
  3.9 0.7 copy-done.7
  4.5 0.0 copy-start.3
  4.5 0.0 copy-start.1
  4.5 0.0 copy-start.5
  4.5 0.0 copy-start.8
  4.5 0.9 %shard_map.55 = (f32[2,1280,128]{2,1,0:T(8,128)S(1)}, f32[1280,128]{1,0:T(8,128)S(1)}, f32[32,8,128]{2,1,0:T(8,128)S(1)}) custom-call(s32[4]{0:T(128)S(1)} %copy-done.7, s32[4,8]{1,0:T(4,128)S(1)} %bitcast.4, f32[1024,512]{1,0:T(8,128)S(1)} %copy-done, f32[4,16,512]{2,1,0:T(8,128)S(1)} %copy-done.2, f32[1,512]{1,0:T(1,128)S(1)} %bitcast.6), custom_call_target="tpu_custom_call" | custom-call | tf_op jit(solution)/shard_map/pallas_call | solution.py:414
  5.5 0.0 copy-done.3
  5.5 62.9 %shard_map.56 = (f32[4,1280,128]{2,1,0:T(8,128)S(1)}, f32[16,4,16,512]{3,2,1,0:T(8,128)S(1)}, f32[16,24,8,128]{3,2,1,0:T(8,128)S(1)}, f32[2,8,128]{2,1,0:T(8,128)S(1)}) custom-call(f32[2,8,160,128]{3,2,1,0:T(8,128)S(1)} %bitcast.3, f32[1280,128]{1,0:T(8,128)S(1)} %get-tuple-element.13.ce, f32[32,8,128]{2,1,0:T(8,128)S(1)} %get-tuple-element.14.gc_hbm, ...), custom_call_target="tpu_custom_call" | custom-call | tf_op jit(solution)/shard_map/pallas_call | solution.py:433
  68.4 0.0 copy-done.1
  68.4 0.0 copy-done.5
  68.4 0.0 copy-done.8
  68.4 8.3 %shard_map.57 = f32[1024,512]{1,0:T(8,128)} custom-call(s32[4]{0:T(128)S(1)} %copy-done.8, s32[4,8]{1,0:T(4,128)S(1)} %bitcast.5, f32[2,8,128]{2,1,0:T(8,128)S(1)} %get-tuple-element.15.refs_2_.refs_3_, f32[2,8,128]{2,1,0:T(8,128)S(1)} %get-tuple-element.15.refs_2_.refs_3_, f32[4,1280,128]{2,1,0:T(8,128)S(1)} %get-tuple-element.16.refs_4_, ...), custom_call_target="tpu_custom_call" | custom-call | tf_op jit(solution)/shard_map/pallas_call | solution.py:468
Async XLA Ops:
  0.0 1.6 %copy-start = (f32[1024,512]{1,0:T(8,128)S(1)}, f32[1024,512]{1,0:T(8,128)}, u32[]{:S(2)}) copy-start(f32[1024,512]{1,0:T(8,128)} %refs_7_.1) | copy-start | bytes 6291460
  1.6 0.9 %copy-start.2 = (f32[4,16,512]{2,1,0:T(8,128)S(1)}, f32[4,16,512]{2,1,0:T(8,128)}, u32[]{:S(2)}) copy-start(f32[4,16,512]{2,1,0:T(8,128)} %f_hbm.3) | copy-start | bytes 393220
  2.5 0.7 copy-start.4
  3.2 0.7 copy-start.6
  3.9 0.7 copy-start.7
  4.5 0.9 %copy-start.3 = (f32[4,16,512]{2,1,0:T(8,128)S(1)}, f32[4,16,512]{2,1,0:T(8,128)}, u32[]{:S(2)}) copy-start(f32[4,16,512]{2,1,0:T(8,128)} %f_hbm.3) | copy-start | bytes 393220
  4.5 63.8 %copy-start.1 = (f32[1024,512]{1,0:T(8,128)S(1)}, f32[1024,512]{1,0:T(8,128)}, u32[]{:S(2)}) copy-start(f32[1024,512]{1,0:T(8,128)} %refs_7_.1) | copy-start | bytes 6291460
  4.5 63.9 %copy-start.5 = (s32[8,4]{0,1:T(4,128)S(1)}, s32[8,4]{0,1:T(4,128)}, u32[]{:S(2)}) copy-start(s32[8,4]{0,1:T(4,128)} %param.6) | copy-start | bytes 388
  4.5 63.9 %copy-start.8 = (s32[4]{0:T(128)S(1)}, s32[4]{0:T(128)}, u32[]{:S(2)}) copy-start(s32[4]{0:T(128)} %refs_0_.1) | copy-start | bytes 52

commit v4 on v3

--- a/solution.py
+++ b/solution.py
@@ -175,7 +175,7 @@
 
     lax.fori_loop(1, NIN, spread_g, 0)
 
-    for dz in FAR + (0,):
+    for dz in NEAR + (0,):
         for dx in range(1, NX):
             part = pl.ds(pl.multiple_of(lax.rem(x + dx, NX) * CH, 8), CH)
             send(m.at[:, lax.rem(z + dz, NZ), part], rb1.at[dz, dx - 1], r1_s, r1_r.at[dz], xdev(dx))
@@ -258,9 +258,8 @@
         send(t_out.at[pl.ds(0, 2), mine], t_out.at[pl.ds(0, 2), mine], ex_s, ex_r, xdev(dx))
 
     mcopy.wait()
-    y_onward(f_out, f_s, f_r, fc_s, fc_r)
-
-    for dz in FAR + (0,):
+
+    for dz in NEAR + (0,):
         wait_for(rb1.at[dz], r1_r.at[dz])
         acc = mq[:, lax.rem(z + dz, NZ)]
         for q in range(NX - 1):
@@ -271,6 +270,7 @@
 
     wait_for(t_out.at[pl.ds(0, 2), pl.ds(0, (NX - 1) * CH)], ex_r)
     round_z(0)
+    y_onward(f_out, f_s, f_r, fc_s, fc_r)
 
     wait_for(gf.at[pl.ds(1, NIN - 1)], gag_r)
     gown = pltpu.make_async_copy(gf.at[pl.ds(0, GROWS)], g_out.at[o], loc.at[3])
@@ -461,7 +461,7 @@
         ),
     )(mids.reshape(2, NZ, NX * CH, TILE), ends, shares, factor_rows)
 
-    rt = 4
+    rt = 2
     br = rt * TILE
     depth = NBLK * 2 * TILE
     bf16 = jnp.bfloat16

time: 76.9 us -> 77 us (level)
  no operation moved by 1% of the time
where the time goes in v4:
time: 77 us; the launch traced here: 76.9 us
  Pallas kernels  72.3 us (94%)
  local copies, waits for them, and re-layouts  4.53 us (6%)
    pallas_call x1, Pallas kernels, body(): pl.pallas_call(exchange, out_shape=(jax.ShapeDtypeStruct((NBLK, ROWS, TIL...  63.3 us
    pallas_call x1, Pallas kernels, body(): pl.pallas_call(lambda *refs: compensate(rt, *refs), out_shape=jax.ShapeDt...  8.09 us
    unnamed x18, local copies, waits for them, and re-layouts  4.53 us

profile of v4, /device:TPU:1, one launch (start us, length us, event | category | flops | bytes accessed | tf_op | source)
XLA Modules:
  0.0 76.9 jit_solution(10535596016388252332)
XLA Ops:
  0.0 0.0 copy-start
  0.0 1.6 %copy-done = f32[1024,512]{1,0:T(8,128)S(1)} copy-done((f32[1024,512]{1,0:T(8,128)S(1)}, f32[1024,512]{1,0:T(8,128)}, u32[]{:S(2)}) %copy-start) | copy-done | bytes 2097176
  1.6 0.0 copy-start.2
  1.6 0.9 %copy-done.2 = f32[4,16,512]{2,1,0:T(8,128)S(1)} copy-done((f32[4,16,512]{2,1,0:T(8,128)S(1)}, f32[4,16,512]{2,1,0:T(8,128)}, u32[]{:S(2)}) %copy-start.2) | copy-done | bytes 131096
  2.5 0.0 copy-start.4
  2.5 0.7 copy-done.4
  3.2 0.0 copy-start.6
  3.2 0.7 copy-done.6
  3.9 0.0 copy-start.7
  3.9 0.7 copy-done.7
  4.5 0.0 copy-start.3
  4.5 0.0 copy-start.1
  4.5 0.0 copy-start.5
  4.5 0.0 copy-start.8
  4.5 0.9 %shard_map.55 = (f32[2,1280,128]{2,1,0:T(8,128)S(1)}, f32[1280,128]{1,0:T(8,128)S(1)}, f32[32,8,128]{2,1,0:T(8,128)S(1)}) custom-call(s32[4]{0:T(128)S(1)} %copy-done.7, s32[4,8]{1,0:T(4,128)S(1)} %bitcast.4, f32[1024,512]{1,0:T(8,128)S(1)} %copy-done, f32[4,16,512]{2,1,0:T(8,128)S(1)} %copy-done.2, f32[1,512]{1,0:T(1,128)S(1)} %bitcast.6), custom_call_target="tpu_custom_call" | custom-call | tf_op jit(solution)/shard_map/pallas_call | solution.py:414
  5.5 0.0 copy-done.3
  5.5 63.3 %shard_map.56 = (f32[4,1280,128]{2,1,0:T(8,128)S(1)}, f32[16,4,16,512]{3,2,1,0:T(8,128)S(1)}, f32[16,24,8,128]{3,2,1,0:T(8,128)S(1)}, f32[2,8,128]{2,1,0:T(8,128)S(1)}) custom-call(f32[2,8,160,128]{3,2,1,0:T(8,128)S(1)} %bitcast.3, f32[1280,128]{1,0:T(8,128)S(1)} %get-tuple-element.13.ce, f32[32,8,128]{2,1,0:T(8,128)S(1)} %get-tuple-element.14.gc_hbm, ...), custom_call_target="tpu_custom_call" | custom-call | tf_op jit(solution)/shard_map/pallas_call | solution.py:433
  68.7 0.0 copy-done.1
  68.8 0.0 copy-done.5
  68.8 0.0 copy-done.8
  68.8 8.1 %shard_map.57 = f32[1024,512]{1,0:T(8,128)} custom-call(s32[4]{0:T(128)S(1)} %copy-done.8, s32[4,8]{1,0:T(4,128)S(1)} %bitcast.5, f32[2,8,128]{2,1,0:T(8,128)S(1)} %get-tuple-element.15.refs_2_.refs_3_, f32[2,8,128]{2,1,0:T(8,128)S(1)} %get-tuple-element.15.refs_2_.refs_3_, f32[4,1280,128]{2,1,0:T(8,128)S(1)} %get-tuple-element.16.refs_4_, ...), custom_call_target="tpu_custom_call" | custom-call | tf_op jit(solution)/shard_map/pallas_call | solution.py:468
Async XLA Ops:
  0.0 1.6 %copy-start = (f32[1024,512]{1,0:T(8,128)S(1)}, f32[1024,512]{1,0:T(8,128)}, u32[]{:S(2)}) copy-start(f32[1024,512]{1,0:T(8,128)} %refs_7_.1) | copy-start | bytes 6291460
  1.6 0.9 %copy-start.2 = (f32[4,16,512]{2,1,0:T(8,128)S(1)}, f32[4,16,512]{2,1,0:T(8,128)}, u32[]{:S(2)}) copy-start(f32[4,16,512]{2,1,0:T(8,128)} %f_hbm.3) | copy-start | bytes 393220
  2.5 0.7 copy-start.4
  3.2 0.7 copy-start.6
  3.9 0.7 copy-start.7
  4.5 0.9 %copy-start.3 = (f32[4,16,512]{2,1,0:T(8,128)S(1)}, f32[4,16,512]{2,1,0:T(8,128)}, u32[]{:S(2)}) copy-start(f32[4,16,512]{2,1,0:T(8,128)} %f_hbm.3) | copy-start | bytes 393220
  4.5 64.2 %copy-start.1 = (f32[1024,512]{1,0:T(8,128)S(1)}, f32[1024,512]{1,0:T(8,128)}, u32[]{:S(2)}) copy-start(f32[1024,512]{1,0:T(8,128)} %refs_7_.1) | copy-start | bytes 6291460
  4.5 64.2 %copy-start.5 = (s32[8,4]{0,1:T(4,128)S(1)}, s32[8,4]{0,1:T(4,128)}, u32[]{:S(2)}) copy-start(s32[8,4]{0,1:T(4,128)} %param.6) | copy-start | bytes 388
  4.5 64.2 %copy-start.8 = (s32[4]{0:T(128)S(1)}, s32[4]{0:T(128)}, u32[]{:S(2)}) copy-start(s32[4]{0:T(128)} %refs_0_.1) | copy-start | bytes 52
